TPU v7x, 32 devices: a whole 2x2x4 slice. The times are simulated.
32 devices in a mesh: grp: 2 (over x), yz: 8 (over z, y), gx: 2 (over core).
Axes of the slice: x: 2, y: 2, z: 4, core: 2. Of those that a mesh axis runs over, the one named last changes fastest.
Arguments:
- hidden: bfloat16 [2, 192, 16384], P(None, ('grp', 'yz'), 'gx'), parts along dimension 1, may hold values from -6 to 6
- w_query: bfloat16 [16384, 8192], P('gx', 'yz'), may hold values from -0.046875 to 0.046875
- key_value_weight: bfloat16 [16384, 1024], P('gx', 'yz'), may hold values from -0.046875 to 0.046875
- w_out: bfloat16 [8192, 16384], P('gx', 'yz'), may hold values from -0.125 to 0.125
- cache_keys: bfloat16 [192, 4, 512, 128], P(('grp', 'yz'), 'gx'), parts along dimension 0, may hold values from -64 to 64
- stored_values: bfloat16 [192, 4, 512, 128], P(('grp', 'yz'), 'gx'), parts along dimension 0, may hold values from -6 to 6
- lengths: int32 [192], P(('grp', 'yz')), parts along dimension 0, may hold values from 1 to 512, 19660 in all
- positions: int32 [192], P(('grp', 'yz')), parts along dimension 0, may hold values from 0 to 8191
Outputs:
- attention_out: bfloat16 [2, 192, 16384], P(None, 'grp', ('yz', 'gx')), parts along dimension 1
- new_entries: bfloat16 [2, 192, 4, 2, 128], P(None, ('grp', 'yz'), 'gx'), parts along dimension 1
There are 2 independent parts, one for each index of `grp`. A program takes and returns all parts, laid end to end along the dimension named above; an argument that names none is the same for every part. Nothing has to cross between parts.
Inputs may be any that keep to these rules, and one draw needn't show every extreme that they name: Row b's caches hold lengths[b] filled slots at the front; in every draw some row fills all 512.
All inputs are finite; a program needn't handle non-finite values. No bound on the sum of `lengths` on one device may be relied on, other than what follows from the above.
Results may differ from a plain program's by a relative error of at most 0.009.
Values may be sent and summed in bfloat16 or wider, within the bound.
A program may use at most 256 MiB of HBM per device.

v0:
```python
import math

import jax
import jax.numpy as jnp
from jax import lax
from jax.sharding import PartitionSpec as P


def rotary(vector, position):
    half_dim = vector.shape[-1] // 2
    freq_index = jnp.arange(half_dim, dtype=jnp.float32)
    inverse_freq = jnp.exp(freq_index * (-2.0 * math.log(500000.0) / vector.shape[-1]))
    phase_angle = position.astype(jnp.float32)[..., None] * inverse_freq
    cosine = jnp.cos(phase_angle)
    sine_part = jnp.sin(phase_angle)
    lower_half = vector[..., :half_dim]
    upper_half = vector[..., half_dim:]
    return jnp.concatenate(
        [
            lower_half * cosine - upper_half * sine_part,
            upper_half * cosine + lower_half * sine_part,
        ],
        axis=-1,
    )


def attend(rotated_query, new_keys, new_values, cache_keys, stored_values, lengths, first_step):
    step_local, row_local, kv_local, group_size, head_dim = rotated_query.shape
    slot_total = cache_keys.shape[2]
    score_scale = head_dim ** (-0.5)
    query_rows = step_local * group_size
    queries = rotated_query.transpose(1, 2, 0, 3, 4).reshape(
        row_local, kv_local, query_rows, head_dim
    )
    fresh_keys = new_keys.transpose(1, 2, 0, 3)
    fresh_values = new_values.transpose(1, 2, 0, 3)
    query_step = first_step + jnp.arange(query_rows) // group_size
    new_scores = (
        jnp.einsum("rhqd,rhtd->rhqt", queries, fresh_keys, preferred_element_type=jnp.float32)
        * score_scale
    )
    step_valid = jnp.arange(fresh_keys.shape[2])[None, :] <= query_step[:, None]
    new_scores = jnp.where(step_valid[None, None, :, :], new_scores, -jnp.inf)
    length_col = lengths[:, None, None, None]
    cache_scores = (
        jnp.einsum("rhqd,rhld->rhql", queries, cache_keys, preferred_element_type=jnp.float32)
        * score_scale
    )
    cache_scores = jnp.where(jnp.arange(slot_total) < length_col, cache_scores, -jnp.inf)
    row_top = jnp.maximum(jnp.max(cache_scores, axis=3), jnp.max(new_scores, axis=3))[..., None]
    cache_exp = jnp.exp(cache_scores - row_top)
    new_exp = jnp.exp(new_scores - row_top)
    denominator = jnp.sum(cache_exp, axis=3, keepdims=True) + jnp.sum(
        new_exp, axis=3, keepdims=True
    )
    cache_weights = (cache_exp / denominator).astype(jnp.bfloat16)
    new_weights = (new_exp / denominator).astype(jnp.bfloat16)
    new_part = jnp.einsum(
        "rhqt,rhtd->rhqd", new_weights, fresh_values, preferred_element_type=jnp.float32
    )
    cache_part = jnp.einsum(
        "rhql,rhld->rhqd", cache_weights, stored_values, preferred_element_type=jnp.float32
    )
    attended = (cache_part + new_part).astype(jnp.bfloat16)
    attended = attended.reshape(row_local, kv_local, step_local, group_size, head_dim)
    return attended.transpose(2, 0, 1, 3, 4)


def body(hidden, w_query, key_value_weight, w_out, cache_keys, stored_values, lengths, positions):
    step_count = hidden.shape[0]
    row_local = hidden.shape[1]
    kv_local = cache_keys.shape[1]
    head_dim = cache_keys.shape[3]
    heads_local = w_out.shape[0] // head_dim
    group_size = heads_local // kv_local
    query_cols = w_query.shape[1]
    output_list = []
    known_entries = None
    for step_index in range(step_count):
        project_segment = lax.all_gather(
            hidden[step_index : step_index + 1], "yz", axis=1, tiled=True
        )
        project_query_part = jnp.einsum(
            "snd,dc->snc", project_segment, w_query, preferred_element_type=jnp.float32
        )
        project_fresh_part = jnp.einsum(
            "snd,dc->snc", project_segment, key_value_weight, preferred_element_type=jnp.float32
        )
        decode_partials = jnp.concatenate([project_query_part, project_fresh_part], axis=2)
        query_part = decode_partials[:, :, :query_cols]
        fresh_part = decode_partials[:, :, query_cols:]
        moved_query = lax.all_to_all(query_part, "yz", split_axis=1, concat_axis=2, tiled=True)
        moved_fresh = lax.all_to_all(fresh_part, "yz", split_axis=1, concat_axis=2, tiled=True)
        query_full = lax.psum_scatter(moved_query, "gx", scatter_dimension=2, tiled=True)
        fresh_full = lax.psum_scatter(moved_fresh, "gx", scatter_dimension=2, tiled=True)
        step_local = query_full.shape[0]
        step_pos = (
            positions[None, :] + (step_index + jnp.arange(step_local, dtype=jnp.int32))[:, None]
        )
        query_heads = query_full.reshape(step_local, row_local, heads_local, head_dim)
        rotated_query = rotary(query_heads, step_pos[:, :, None]).astype(jnp.bfloat16)
        rotated_query = rotated_query.reshape(step_local, row_local, kv_local, group_size, head_dim)
        fresh_heads = fresh_full.reshape(step_local, row_local, kv_local, 2, head_dim)
        new_key = rotary(fresh_heads[:, :, :, 0], step_pos[:, :, None])
        entries = jnp.stack([new_key, fresh_heads[:, :, :, 1]], axis=3).astype(jnp.bfloat16)
        known = (
            entries if known_entries is None else jnp.concatenate([known_entries, entries], axis=0)
        )
        attended = attend(
            rotated_query,
            known[:, :, :, 0],
            known[:, :, :, 1],
            cache_keys,
            stored_values,
            lengths,
            step_index,
        )
        attended = attended.reshape(step_local, row_local, heads_local * head_dim)
        mixed_cols = jnp.einsum(
            "snc,cd->snd",
            lax.all_gather(attended, "yz", axis=1, tiled=True),
            w_out,
            preferred_element_type=jnp.float32,
        )
        output_block = lax.psum_scatter(mixed_cols, "gx", scatter_dimension=2, tiled=True).astype(
            jnp.bfloat16
        )
        output_block, known_entries = (output_block, known)
        output_list.append(output_block)
    attention_out = jnp.concatenate(output_list, axis=0)
    return (attention_out, known_entries)


def solution(mesh):
    placed = (
        P(None, ("grp", "yz"), "gx"),
        P("gx", "yz"),
        P("gx", "yz"),
        P("gx", "yz"),
        P(("grp", "yz"), "gx", None, None),
        P(("grp", "yz"), "gx", None, None),
        P(("grp", "yz")),
        P(("grp", "yz")),
    )
    return jax.shard_map(
        body,
        mesh=mesh,
        in_specs=placed,
        out_specs=(P(None, "grp", ("yz", "gx")), P(None, ("grp", "yz"), "gx", None, None)),
        check_vma=False,
    )
```

profile of v0, /device:TPU:1, one launch (start us, length us, event | category | flops | bytes accessed | tf_op | source)
XLA Modules:
  0.0 536.8 jit_solution(4249159802898013961)
XLA Ops:
  15.1 57.2 %all-gather.5.cloned.1.call-done = bf16[1,96,8192]{2,0,1:T(2,128)(2,1)} async-done(((bf16[1,12,8192]{2,0,1:T(2,128)(2,1)}), bf16[1,96,8192]{2,0,1:T(2,128)(2,1)}) %all-gather.5.cloned.1.call-update) | async-done | bytes 1572880 | tf_op jit(solution)/shard_map/all_gather | solution.py:80
  72.3 5.1 fusion
  81.5 11.1 %fusion.13 = f32[1,96,1024]{2,1,0:T(8,128)S(1)} fusion(bf16[8192,1024]{1,0:T(8,128)(2,1)} %param.9, bf16[1,96,8192]{2,0,1:T(2,128)(2,1)} %all-gather.5.cloned.1.call-done), kind=kOutput, calls=%fused_computation.23 | convolution fusion | flops 1610612736 | bytes 18743296 | tf_op jit(solution)/shard_map/snd,dc->snc/dot_general | solution.py:83
  92.6 42.0 %all-gather.3.cloned.1.call-done = bf16[1,96,8192]{2,0,1:T(2,128)(2,1)} async-done(((bf16[1,12,8192]{2,0,1:T(2,128)(2,1)}), bf16[1,96,8192]{2,0,1:T(2,128)(2,1)}) %all-gather.3.cloned.1.call-update) | async-done | bytes 1572880 | tf_op jit(solution)/shard_map/all_gather | solution.py:80
  134.6 10.9 %fusion.10 = f32[1,96,1024]{2,1,0:T(8,128)S(1)} fusion(bf16[8192,1024]{1,0:T(8,128)(2,1)} %param.9, bf16[1,96,8192]{2,0,1:T(2,128)(2,1)} %all-gather.3.cloned.1.call-done), kind=kOutput, calls=%fused_computation.22 | convolution fusion | flops 1610612736 | bytes 18743296 | tf_op jit(solution)/shard_map/snd,dc->snc/dot_general | solution.py:83
  155.3 5.9 %copy.73 = f32[1,12,1024]{0,1,2:T(8,128)} copy(f32[1,12,1024]{2,0,1:T(1,128)S(1)} %bitcast.134) | data formatting | bytes 98304
  161.2 6.5 %bitcast_reduce_fusion.2 = f32[1024,12]{1,0:T(8,128)} fusion(f32[1,12,1024]{0,1,2:T(8,128)} %copy.73), kind=kLoop, calls=%fused_computation.4 | loop fusion | bytes 98304
  168.3 5.4 %all-to-all-start.2 = ((f32[1,96,1024]{2,0,1:T(1,128)}), f32[1,96,1024]{2,0,1:T(1,128)S(1)}, u32[]{:S(2)}, u32[]{:S(2)}) async-start(f32[1,96,1024]{2,0,1:T(1,128)} %copy.56), calls=%async_computation.3 | async-start | bytes 786432 | tf_op jit(solution)/shard_map/all_to_all | solution.py:92
  175.2 6.5 %copy.69 = f32[1,12,1024]{0,1,2:T(8,128)} copy(f32[1,12,1024]{2,0,1:T(1,128)} %bitcast.135) | data formatting | bytes 98304
  181.7 6.5 %bitcast_reduce_fusion.3 = f32[1024,12]{1,0:T(8,128)} fusion(f32[1,12,1024]{0,1,2:T(8,128)} %copy.69), kind=kLoop, calls=%fused_computation.5 | loop fusion | bytes 98304
  211.3 5.6 %all-to-all-start = ((f32[1,96,1024]{2,0,1:T(1,128)}), f32[1,96,1024]{2,0,1:T(1,128)}, u32[]{:S(2)}, u32[]{:S(2)}) async-start(f32[1,96,1024]{2,0,1:T(1,128)} %copy.50), calls=%async_computation | async-start | bytes 786432 | tf_op jit(solution)/shard_map/all_to_all | solution.py:92
  220.2 37.6 %reshape.420 = f32[1,12,8192]{0,1,2:T(8,128)} reshape(f32[1,12,8,1024]{1,3,2,0:T(8,128)} %copy.76) | data formatting | bytes 786432
  257.8 23.8 %bitcast_reduce_fusion = f32[8192,12]{1,0:T(8,128)} fusion(f32[1,12,8192]{0,1,2:T(8,128)} %reshape.420), kind=kLoop, calls=%fused_computation | loop fusion | bytes 786432
  286.2 37.6 %reshape.419 = f32[1,12,8192]{0,1,2:T(8,128)} reshape(f32[1,12,8,1024]{1,3,2,0:T(8,128)} %copy.75) | data formatting | bytes 786432
  323.7 23.8 %bitcast_reduce_fusion.1 = f32[8192,12]{1,0:T(8,128)} fusion(f32[1,12,8192]{0,1,2:T(8,128)} %reshape.419), kind=kLoop, calls=%fused_computation.1 | loop fusion | bytes 786432
  347.6 16.8 %reshape_bitcast_fusion = f32[1,12,4096]{0,1,2:T(8,128)} fusion(f32[4096,12]{1,0:T(8,128)} %reduce-scatter.23.cloned.1.call-done), kind=kLoop, calls=%fused_computation.2 | loop fusion | bytes 393216
  364.5 18.7 %copy.72 = f32[1,12,4096]{2,0,1:T(1,128)S(1)} copy(f32[1,12,4096]{0,1,2:T(8,128)} %reshape_bitcast_fusion) | data formatting | bytes 393216
  383.2 16.8 %reshape_bitcast_fusion.1 = f32[1,12,4096]{0,1,2:T(8,128)} fusion(f32[4096,12]{1,0:T(8,128)} %reduce-scatter.19.cloned.1.call-done), kind=kLoop, calls=%fused_computation.3 | loop fusion | bytes 393216
  400.0 18.7 %copy.68 = f32[1,12,4096]{2,0,1:T(1,128)S(1)} copy(f32[1,12,4096]{0,1,2:T(8,128)} %reshape_bitcast_fusion.1) | data formatting | bytes 393216
  423.9 33.1 %all_gather.15 = bf16[1,96,4096]{2,0,1:T(2,128)(2,1)S(1)} all-gather(bf16[1,12,4096]{2,0,1:T(2,128)(2,1)S(1)} %reshape_transpose_reshape.11), channel_id=1, replica_groups=mesh['grp'=2,'yz'=8,'gx'=2] {'yz'}, dimensions={1}, use_global_device_ids=true | all-gather | bytes 884736 | tf_op jit(solution)/shard_map/all_gather | solution.py:121
  457.0 10.2 %convolution_bitcast_fusion = f32[1,96,2048]{2,1,0:T(8,128)} fusion(bf16[4096,2048]{1,0:T(8,128)(2,1)} %param.11, bf16[1,96,4096]{2,0,1:T(2,128)(2,1)S(1)} %all_gather.15), kind=kOutput, calls=%fused_computation.8 | convolution fusion | flops 1610612736 | bytes 18350080 | tf_op jit(solution)/shard_map/snc,cd->snd/dot_general | solution.py:119
  470.1 32.4 %all_gather.13 = bf16[1,96,4096]{2,0,1:T(2,128)(2,1)S(1)} all-gather(bf16[1,12,4096]{2,0,1:T(2,128)(2,1)S(1)} %reshape_transpose_reshape.10), channel_id=1, replica_groups=mesh['grp'=2,'yz'=8,'gx'=2] {'yz'}, dimensions={1}, use_global_device_ids=true | all-gather | bytes 884736 | tf_op jit(solution)/shard_map/all_gather | solution.py:121
  502.5 10.2 %convolution_bitcast_fusion.1 = f32[1,96,2048]{2,1,0:T(8,128)} fusion(bf16[4096,2048]{1,0:T(8,128)(2,1)} %param.11, bf16[1,96,4096]{2,0,1:T(2,128)(2,1)S(1)} %all_gather.13), kind=kOutput, calls=%fused_computation.9 | convolution fusion | flops 1610612736 | bytes 18350080 | tf_op jit(solution)/shard_map/snc,cd->snd/dot_general | solution.py:119
  514.3 13.6 %reduce-scatter.15.cloned.1.call-done = f32[1,96,1024]{2,1,0:T(8,128)} async-done(((f32[1,96,2048]{2,1,0:T(8,128)}), f32[1,96,1024]{2,1,0:T(8,128)}) %reduce-scatter.15.cloned.1.call-update) | async-done | bytes 393232 | tf_op jit(solution)/shard_map/reduce_scatter | solution.py:125
  (110 shorter events, 66.2 us)
Async XLA Ops:
  7.2 414.3 %copy-start = (bf16[12,2,512,128]{3,2,1,0:T(8,128)(2,1)S(1)}, bf16[12,2,512,128]{3,2,1,0:T(8,128)(2,1)}, u32[]{:S(2)}) copy-start(bf16[12,2,512,128]{3,2,1,0:T(8,128)(2,1)} %param.12) | copy-start | bytes 9437188
  7.2 65.1 %all-gather.5.cloned.1.call-start = ((), (), s32[]{:S(2)}) async-start(), calls=%async_computation.12 | async-start | bytes 3538944 | tf_op jit(solution)/shard_map/all_gather | solution.py:80
  10.4 124.2 %all-gather.3.cloned.1.call-start = ((), (), s32[]{:S(2)}) async-start(), calls=%async_computation.10 | async-start | bytes 3538944 | tf_op jit(solution)/shard_map/all_gather | solution.py:80
  77.4 73.1 %all-to-all-start.3 = ((f32[1,96,128]{2,0,1:T(1,128)}), f32[1,96,128]{2,0,1:T(1,128)}, u32[]{:S(2)}, u32[]{:S(2)}) async-start(f32[1,96,128]{2,0,1:T(1,128)} %bitcast.27), calls=%async_computation.4 | async-start | bytes 98304 | tf_op jit(solution)/shard_map/all_to_all | solution.py:93
  134.6 10.9 %copy-start.1 = (bf16[8192,128]{1,0:T(8,128)(2,1)S(1)}, bf16[8192,128]{1,0:T(8,128)(2,1)}, u32[]{:S(2)}) copy-start(bf16[8192,128]{1,0:T(8,128)(2,1)} %param.10) | copy-start | bytes 6291460
  134.6 10.9 %copy-start.2 = (bf16[1,96,8192]{2,0,1:T(2,128)(2,1)S(1)}, bf16[1,96,8192]{2,0,1:T(2,128)(2,1)}, u32[]{:S(2)}) copy-start(bf16[1,96,8192]{2,0,1:T(2,128)(2,1)} %all-gather.3.cloned.1.call-done) | copy-start | bytes 4718596
  150.4 17.3 %all-to-all-start.1 = ((f32[1,96,128]{2,0,1:T(1,128)}), f32[1,96,128]{2,0,1:T(1,128)S(1)}, u32[]{:S(2)}, u32[]{:S(2)}) async-start(f32[1,96,128]{2,0,1:T(1,128)} %bitcast.133), calls=%async_computation.1 | async-start | bytes 98304 | tf_op jit(solution)/shard_map/all_to_all | solution.py:93
  154.3 34.0 %reduce-scatter.25.cloned.1.call-start = ((), (), s32[]{:S(2)}) async-start(), calls=%async_computation.17 | async-start | bytes 786432
  168.3 43.0 %all-to-all-start.2 = ((f32[1,96,1024]{2,0,1:T(1,128)}), f32[1,96,1024]{2,0,1:T(1,128)S(1)}, u32[]{:S(2)}, u32[]{:S(2)}) async-start(f32[1,96,1024]{2,0,1:T(1,128)} %copy.56), calls=%async_computation.3 | async-start | bytes 786432 | tf_op jit(solution)/shard_map/all_to_all | solution.py:92
  173.7 25.2 %reduce-scatter.21.cloned.1.call-start = ((), (), s32[]{:S(2)}) async-start(), calls=%async_computation.15 | async-start | bytes 786432
  211.3 70.8 %all-to-all-start = ((f32[1,96,1024]{2,0,1:T(1,128)}), f32[1,96,1024]{2,0,1:T(1,128)}, u32[]{:S(2)}, u32[]{:S(2)}) async-start(f32[1,96,1024]{2,0,1:T(1,128)} %copy.50), calls=%async_computation | async-start | bytes 786432 | tf_op jit(solution)/shard_map/all_to_all | solution.py:92
  216.9 130.7 %reduce-scatter.23.cloned.1.call-start = ((), (), s32[]{:S(2)}) async-start(), calls=%async_computation.16 | async-start | bytes 6291456
  281.6 101.6 %reduce-scatter.19.cloned.1.call-start = ((), (), s32[]{:S(2)}) async-start(), calls=%async_computation.14 | async-start | bytes 6291456
  347.6 165.8 %reduce-scatter.17.cloned.1.call-start = ((), (), s32[]{:S(2)}) async-start(), calls=%async_computation.13 | async-start | bytes 1179648 | tf_op jit(solution)/shard_map/reduce_scatter | solution.py:125
  400.0 18.7 %copy-start.9 = (f32[12,64]{1,0:T(8,128)S(1)}, f32[12,64]{1,0:T(8,128)}, u32[]{:S(2)}) copy-start(f32[12,64]{1,0:T(8,128)} %get-tuple-element.26) | copy-start | bytes 9220
  400.0 21.5 %copy-start.8 = (pred[12,512]{1,0:T(8,128)(4,1)S(1)}, pred[12,512]{1,0:T(8,128)(4,1)}, u32[]{:S(2)}) copy-start(pred[12,512]{1,0:T(8,128)(4,1)} %iota_compare_fusion) | copy-start | bytes 18436
  418.8 4.2 copy-start.6
  420.4 2.9 copy-start.13
  457.0 10.5 %copy-start.3 = (bf16[1,12,32,64]{3,2,0,1:T(8,128)(2,1)S(1)}, bf16[1,12,32,64]{3,2,0,1:T(8,128)(2,1)}, u32[]{:S(2)}) copy-start(bf16[1,12,32,64]{3,2,0,1:T(8,128)(2,1)} %get-tuple-element.40) | copy-start | bytes 147460
  457.0 10.5 %copy-start.4 = (bf16[1,12,32,64]{3,2,0,1:T(8,128)(2,1)S(1)}, bf16[1,12,32,64]{3,2,0,1:T(8,128)(2,1)}, u32[]{:S(2)}) copy-start(bf16[1,12,32,64]{3,2,0,1:T(8,128)(2,1)} %get-tuple-element.41) | copy-start | bytes 147460
  467.2 2.0 copy-start.10
  467.2 60.7 %reduce-scatter.15.cloned.1.call-start = ((), (), s32[]{:S(2)}) async-start(), calls=%async_computation.11 | async-start | bytes 1179648 | tf_op jit(solution)/shard_map/reduce_scatter | solution.py:125
  467.5 1.9 copy-start.14
  502.5 10.2 %copy-start.7 = (bf16[2,12,2,2,128]{4,0,2,1,3:T(2,128)(2,1)S(1)}, bf16[2,12,2,2,128]{4,0,2,1,3:T(2,128)(2,1)}, u32[]{:S(2)}) copy-start(bf16[2,12,2,2,128]{4,0,2,1,3:T(2,128)(2,1)} %maximum_maximum_fusion) | copy-start | bytes 73732
  (3 other events, 3.6 us)
Sparse Core Ops, SparseCore 0:
  10.6 61.6 all-gather.4
  75.0 59.5 all-gather.2
  167.8 9.9 reduce-scatter.24
  188.4 10.4 reduce-scatter.20
  281.7 13.6 reduce-scatter.22
  347.7 13.6 reduce-scatter.18
  467.4 12.1 reduce-scatter.16
  512.8 15.0 reduce-scatter.14
where the time goes:
time: 543 us; the launch traced here: 537 us
  local copies, waits for them, and re-layouts  253 us (47%)
  waiting for transfers between devices  116 us (21%)
  blocking collectives  65.5 us (12%)
  matrix products  55.1 us (10%)
  starting transfers between devices  20.1 us (4%)
  between operations  14.7 us (3%)
  other arithmetic  12.1 us (2%)
    unnamed x50, local copies, waits for them, and re-layouts  242 us
    all_gather x2, waiting for transfers between devices, body(): lax.all_gather(hidden[step_index:step_index + 1], 'yz', axis=1, tiled=True)  99.1 us
    all_gather x2, blocking collectives, body(): lax.all_gather(attended, 'yz', axis=1, tiled=True)  65.5 us
    dot_general x2, matrix products, body(): jnp.einsum('snd,dc->snc', project_segment, w_query, preferred_element_typ...  22.1 us
    dot_general x2, matrix products, body(): jnp.einsum('snc,cd->snd', lax.all_gather(attended, 'yz', axis=1, tiled=Tr...  20.4 us
    reduce_scatter x2, waiting for transfers between devices, body(): lax.psum_scatter(mixed_cols, 'gx', scatter_dimension=2, tiled=True)  13.6 us
    all_to_all x2, starting transfers between devices, body(): lax.all_to_all(query_part, 'yz', split_axis=1, concat_axis=2, tiled=True)  11 us
  transfers between devices with their start and end apart: 12, of which 4 were waited for; matrix products, arithmetic and copies ran while one was open for 49% of the time, Pallas kernels for 0%

commit v1 on v0

v1 whole, which is shorter than its diff:
```python
import functools
import math

import jax
import jax.numpy as jnp
from jax import lax
from jax.experimental import pallas as pl
from jax.experimental.pallas import tpu as pltpu
from jax.sharding import PartitionSpec as P

MESH = pl.DeviceIdType.MESH
VMEM_BYTES = 56 * 1024 * 1024


def remote(src, dst, send, recv, **where):
    return pltpu.make_async_remote_copy(
        src_ref=src, dst_ref=dst, send_sem=send, recv_sem=recv, device_id=where, device_id_type=MESH
    )


def enter(n):
    me, core = lax.axis_index("yz"), lax.axis_index("gx")
    barrier = pltpu.get_barrier_semaphore()
    for k in range(1, 2 * n):
        there = lax.rem(me * 2 + core + k, 2 * n)
        pl.semaphore_signal(
            barrier,
            inc=1,
            device_id={"yz": lax.div(there, 2), "gx": lax.rem(there, 2)},
            device_id_type=MESH,
        )
    pl.semaphore_wait(barrier, 2 * n - 1)


class Gather:
    def __init__(self, ny, n, x, xg, own, send, recv):
        self.ny, self.nz, self.n = ny, n // ny, n
        self.x, self.xg, self.own, self.send, self.recv = x, xg, own, send, recv
        self.me = lax.axis_index("yz")
        self.z, self.y = lax.div(self.me, ny), lax.rem(self.me, ny)
        self.chunks = x.shape[0]

    def load(self, c):
        return pltpu.make_async_copy(self.x.at[c], self.xg.at[c, self.me], self.own.at[c])

    def copy(self, c, d, way):
        to = {0: self.me + 1 - 2 * self.y, 1: self.me + self.ny, 2: self.me - self.ny}[way]
        block = self.xg.at[c, d]
        return remote(block, block, self.send.at[c, d, way], self.recv.at[c, d], yz=to)

    def await_block(self, c, d):
        block = self.xg.at[c, d]
        remote(block, block, self.send.at[c, d, 0], self.recv.at[c, d], yz=self.me).wait_recv()

    def ways(self, c, act):
        self.own_sends(c, act)
        for s in range(1, self.nz):
            self.hop_sends(c, s, 1, act)
            self.hop_sends(c, s, -1, act)

    def own_sends(self, c, act):
        @pl.when(self.z + 1 < self.nz)
        def _():
            act(self.copy(c, self.me, 1))

        @pl.when(self.z > 0)
        def _():
            act(self.copy(c, self.me, 2))

        if self.ny == 2:
            act(self.copy(c, self.me, 0))

    def hop_sends(self, c, s, sign, act, first=None):
        origin = self.z - sign * s
        d = origin * self.ny + self.y

        @pl.when((origin >= 0) & (origin < self.nz))
        def _():
            if first is not None:
                first(d)
            onward = self.z + sign

            @pl.when((onward >= 0) & (onward < self.nz))
            def _():
                act(self.copy(c, d, 1 if sign > 0 else 2))

            if self.ny == 2:
                act(self.copy(c, d, 0))

    def begin(self, c):
        self.load(c).wait()
        self.own_sends(c, lambda copy: copy.start())

    def pass_on(self, c):
        for s in range(1, self.nz):
            for sign in (1, -1):
                self.hop_sends(
                    c, s, sign, lambda copy: copy.start(), lambda d: self.await_block(c, d)
                )

    def across(self, c):
        if self.ny == 2:
            for z in range(self.nz):
                self.await_block(c, z * 2 + 1 - self.y)

    def finish(self):
        for c in range(self.chunks):
            self.ways(c, lambda copy: copy.wait_send())

    def run(self, compute):
        for c in range(self.chunks):
            self.load(c).start()
        enter(self.n)
        self.begin(0)
        for c in range(self.chunks):
            if c + 1 < self.chunks:
                self.begin(c + 1)
            self.pass_on(c)
            if c > 0:
                self.across(c - 1)
                compute(c - 1)
        self.across(self.chunks - 1)
        compute(self.chunks - 1)


def rows_of(xg, c, first, count, half):
    rows = xg.shape[2] // 2
    block = xg[c, pl.ds(first, count)]
    block = block.astype(jnp.float32)[:, half * rows : (half + 1) * rows, :]
    return block.reshape(count * rows, xg.shape[3]).astype(jnp.bfloat16)


def project_kernel(
    ny, n, x, tab, w_q, w_kv, q_out, kv_out,
    xg, tabs, wq, wkv, acc_q, acc_kv, got_q, got_kv, q_send, kv_send, q_recv, kv_recv,
    own, send, recv, w_sem, t_send, t_recv, p_send, p_recv, a_send, a_recv,
):
    me, core = lax.axis_index("yz"), lax.axis_index("gx")
    half = n // 2
    chunks, kc = x.shape[0], x.shape[2]
    rows = x.shape[1] // 2
    depth = w_q.shape[0]
    mine, other = core * half, (1 - core) * half
    side = lax.div(me, half)

    def weight(c, h, which):
        part = pl.ds(h * (depth // 2) + c * kc, kc)
        src, dst = ((w_q, wq), (w_kv, wkv))[which]
        return pltpu.make_async_copy(src.at[part], dst.at[part], w_sem.at[c, h, which])

    for c in range(chunks):
        for h in range(2):
            for which in range(2):
                weight(c, h, which).start()

    gather = Gather(ny, n, x, xg, own, send, recv)

    def tab_copy(k):
        to = lax.rem(me + k, n)
        return remote(tab, tabs.at[lax.rem(me, half)], t_send.at[k - 1], t_recv.at[lax.rem(me, half)], yz=to)

    def product(c, first, at):
        total_q = total_kv = None
        for h in range(2):
            part = pl.ds(h * (depth // 2) + c * kc, kc)
            lhs = rows_of(xg, c, first, half, h)
            term_q = jnp.dot(lhs, wq[part, :], preferred_element_type=jnp.float32)
            term_kv = jnp.dot(lhs, wkv[part, :], preferred_element_type=jnp.float32)
            total_q = term_q if h == 0 else total_q + term_q
            total_kv = term_kv if h == 0 else total_kv + term_kv
        if c == 0:
            acc_q[at] = total_q
            acc_kv[at] = total_kv
        else:
            acc_q[at] += total_q
            acc_kv[at] += total_kv

    swap_q = remote(acc_q.at[1], got_q, p_send.at[0], p_recv.at[0], gx=1 - core)
    swap_kv = remote(acc_kv.at[1], got_kv, p_send.at[1], p_recv.at[1], gx=1 - core)

    def compute(c):
        for h in range(2):
            for which in range(2):
                weight(c, h, which).wait()
        if c == 0:
            @pl.when(side == core)
            def _():
                tabs[lax.rem(me, half)] = tab[...]
                for k in range(1, n):
                    tab_copy(k).start()
        product(c, other, 1)
        if c == chunks - 1:
            swap_q.start()
            swap_kv.start()
        product(c, mine, 0)

    gather.run(compute)

    for i in range(half):
        @pl.when(mine + i != me)
        def _():
            remote(tab, tabs.at[i], t_send.at[0], t_recv.at[i], yz=me).wait_recv()

    swap_q.wait_recv()
    swap_kv.wait_recv()
    heads = wq.shape[1] // 128

    def q_copy(i):
        return remote(
            q_send.at[i], q_recv.at[lax.rem(me, half)], a_send.at[0, i], a_recv.at[0, lax.rem(me, half)],
            yz=mine + i, gx=side,
        )

    def kv_copy(i):
        return remote(
            kv_send.at[i], kv_recv.at[lax.rem(me, half)], a_send.at[1, i], a_recv.at[1, lax.rem(me, half)],
            yz=mine + i, gx=side,
        )

    for i in range(half):
        part = slice(i * rows, (i + 1) * rows)
        cosine = tabs[i, :, :128]
        sine = tabs[i, :, 128:]
        turned = []
        for head in range(heads):
            cols = slice(head * 128, (head + 1) * 128)
            u = acc_q[0, part, cols] + got_q[part, cols]
            turned.append(u * cosine + pltpu.roll(u, 64, 1) * sine)
            if head % 2 == 1:
                pair = jnp.concatenate(turned[-2:], axis=0).astype(jnp.bfloat16)
                q_send[i, pl.ds((head - 1) * rows, 2 * rows), :] = pair
        kv_send[i] = acc_kv[0, part, :] + got_kv[part, :]
        here = (mine + i == me) & (side == core)

        @pl.when(jnp.logical_not(here))
        def _():
            q_copy(i).start()
            kv_copy(i).start()

        @pl.when(here)
        def _():
            q_recv[lax.rem(me, half)] = q_send[i]
            kv_recv[lax.rem(me, half)] = kv_send[i]

    for j in range(half):
        @pl.when(jnp.logical_not((mine + j == me) & (side == core)))
        def _():
            remote(q_send.at[0], q_recv.at[j], a_send.at[0, 0], a_recv.at[0, j], yz=me).wait_recv()
            remote(kv_send.at[0], kv_recv.at[j], a_send.at[1, 0], a_recv.at[1, j], yz=me).wait_recv()

    q_out[...] = q_recv[...]
    kv_out[...] = kv_recv[...]

    gather.finish()
    swap_q.wait_send()
    swap_kv.wait_send()

    @pl.when(side == core)
    def _():
        for k in range(1, n):
            tab_copy(k).wait_send()

    for i in range(half):
        @pl.when(jnp.logical_not((mine + i == me) & (side == core)))
        def _():
            q_copy(i).wait_send()
            kv_copy(i).wait_send()


def project(ny, n, x, tab, w_q, w_kv):
    chunks, rows2, kc = x.shape
    rows, half = rows2 // 2, n // 2
    depth, qcols = w_q.shape
    kvcols = w_kv.shape[1]
    heads = qcols // 128
    f32, bf16 = jnp.float32, jnp.bfloat16
    dma = pltpu.SemaphoreType.DMA
    vmem = pl.BlockSpec(memory_space=pltpu.VMEM)
    hbm = pl.BlockSpec(memory_space=pl.ANY)
    return pl.pallas_call(
        functools.partial(project_kernel, ny, n),
        out_shape=(
            jax.ShapeDtypeStruct((half, heads * rows, 128), bf16),
            jax.ShapeDtypeStruct((half, rows, kvcols), f32),
        ),
        in_specs=[hbm, vmem, hbm, hbm],
        out_specs=(vmem, vmem),
        scratch_shapes=[
            pltpu.VMEM((chunks, n, rows2, kc), bf16),
            pltpu.VMEM((half, rows, 256), f32),
            pltpu.VMEM((depth, qcols), bf16),
            pltpu.VMEM((depth, kvcols), bf16),
            pltpu.VMEM((2, half * rows, qcols), f32),
            pltpu.VMEM((2, half * rows, kvcols), f32),
            pltpu.VMEM((half * rows, qcols), f32),
            pltpu.VMEM((half * rows, kvcols), f32),
            pltpu.VMEM((half, heads * rows, 128), bf16),
            pltpu.VMEM((half, rows, kvcols), f32),
            pltpu.VMEM((half, heads * rows, 128), bf16),
            pltpu.VMEM((half, rows, kvcols), f32),
            dma((chunks,)),
            dma((chunks, n, 3)),
            dma((chunks, n)),
            dma((chunks, 2, 2)),
            dma((n - 1,)),
            dma((half,)),
            dma((2,)),
            dma((2,)),
            dma((2, half)),
            dma((2, half)),
        ],
        compiler_params=pltpu.CompilerParams(
            collective_id=0, has_side_effects=True, vmem_limit_bytes=VMEM_BYTES
        ),
        cost_estimate=pl.CostEstimate(
            flops=2 * n * rows * depth * (qcols + kvcols),
            bytes_accessed=2 * depth * (qcols + kvcols),
            transcendentals=0,
        ),
    )(x, tab, w_q, w_kv)


def mix_kernel(ny, n, x, w, out, xg, wv, acc, got, own, send, recv, w_sem, p_send, p_recv):
    core = lax.axis_index("gx")
    chunks, kc = x.shape[0], x.shape[2]
    depth, cols = w.shape[0], w.shape[1] // 2

    def weight(c, h):
        part = pl.ds(h * (depth // 2) + c * kc, kc)
        return pltpu.make_async_copy(w.at[part], wv.at[part], w_sem.at[c, h])

    for c in range(chunks):
        for h in range(2):
            weight(c, h).start()

    gather = Gather(ny, n, x, xg, own, send, recv)
    swap = remote(acc.at[1], got, p_send.at[0], p_recv.at[0], gx=1 - core)

    def product(c, lhs, first, at):
        columns = pl.ds(pl.multiple_of(first, 128), cols)
        total = None
        for h in range(2):
            part = pl.ds(h * (depth // 2) + c * kc, kc)
            term = jnp.dot(lhs[h], wv[part, columns], preferred_element_type=jnp.float32)
            total = term if h == 0 else total + term
        if c == 0:
            acc[at] = total
        else:
            acc[at] += total

    def compute(c):
        for h in range(2):
            weight(c, h).wait()
        lhs = [rows_of(xg, c, 0, n, h) for h in range(2)]
        product(c, lhs, (1 - core) * cols, 1)
        if c == chunks - 1:
            swap.start()
        product(c, lhs, core * cols, 0)

    gather.run(compute)
    swap.wait_recv()
    out[...] = (acc[0] + got[...]).astype(out.dtype)
    gather.finish()
    swap.wait_send()


def mix(ny, n, x, w):
    chunks, rows2, kc = x.shape
    total = n * rows2 // 2
    depth, width = w.shape
    f32, bf16 = jnp.float32, jnp.bfloat16
    dma = pltpu.SemaphoreType.DMA
    vmem = pl.BlockSpec(memory_space=pltpu.VMEM)
    hbm = pl.BlockSpec(memory_space=pl.ANY)
    return pl.pallas_call(
        functools.partial(mix_kernel, ny, n),
        out_shape=jax.ShapeDtypeStruct((total, width // 2), bf16),
        in_specs=[hbm, hbm],
        out_specs=vmem,
        scratch_shapes=[
            pltpu.VMEM((chunks, n, rows2, kc), bf16),
            pltpu.VMEM((depth, width), bf16),
            pltpu.VMEM((2, total, width // 2), f32),
            pltpu.VMEM((total, width // 2), f32),
            dma((chunks,)),
            dma((chunks, n, 3)),
            dma((chunks, n)),
            dma((chunks, 2)),
            dma((1,)),
            dma((1,)),
        ],
        compiler_params=pltpu.CompilerParams(
            collective_id=1, has_side_effects=True, vmem_limit_bytes=VMEM_BYTES
        ),
        cost_estimate=pl.CostEstimate(
            flops=2 * total * depth * width, bytes_accessed=2 * depth * width, transcendentals=0
        ),
    )(x, w)


def attend_kernel(lengths, q, entries, keys, values, out):
    per_step, kv_local, query_rows, head_dim = q.shape
    slots = keys.shape[2]
    scale = head_dim ** (-0.5)
    f32 = jnp.float32
    base = pl.program_id(0) * per_step
    slot = lax.broadcasted_iota(jnp.int32, (query_rows, slots), 1)
    first = lax.broadcasted_iota(jnp.int32, (query_rows, 1), 0) < query_rows // 2
    for b in range(per_step):
        valid = slot < lengths[base + b]
        for h in range(kv_local):
            query = q[b, h]
            scores = lax.dot_general(
                query, keys[b, h], (((1,), (1,)), ((), ())), preferred_element_type=f32
            ) * scale
            scores = jnp.where(valid, scores, -jnp.inf)
            wide = query.astype(f32)
            fresh = entries[b, h]
            new0 = jnp.sum(wide * fresh[0:1], axis=1, keepdims=True) * scale
            new1 = jnp.sum(wide * fresh[1:2], axis=1, keepdims=True) * scale
            new1 = jnp.where(first, -jnp.inf, new1)
            top = jnp.maximum(jnp.max(scores, axis=1, keepdims=True), jnp.maximum(new0, new1))
            grown = jnp.exp(scores - top)
            grown0, grown1 = jnp.exp(new0 - top), jnp.exp(new1 - top)
            total = jnp.sum(grown, axis=1, keepdims=True) + (grown0 + grown1)
            weights = (grown / total).astype(jnp.bfloat16)
            weight0 = (grown0 / total).astype(jnp.bfloat16).astype(f32)
            weight1 = (grown1 / total).astype(jnp.bfloat16).astype(f32)
            result = jnp.dot(weights, values[b, h], preferred_element_type=f32)
            result = result + (weight0 * fresh[2:3] + weight1 * fresh[3:4])
            out[b, h] = result.astype(out.dtype)


def attend(lengths, q, entries, keys, values):
    rows, kv_local, query_rows, head_dim = q.shape
    slots = keys.shape[2]
    per_step = next(k for k in (3, 4, 2, 1) if rows % k == 0)

    def block(*shape):
        return pl.BlockSpec((per_step, *shape), lambda i: (i,) + (0,) * len(shape))

    return pl.pallas_call(
        attend_kernel,
        grid=(rows // per_step,),
        out_shape=jax.ShapeDtypeStruct(q.shape, jnp.bfloat16),
        in_specs=[
            pl.BlockSpec(memory_space=pltpu.SMEM),
            block(kv_local, query_rows, head_dim),
            block(kv_local, entries.shape[2], head_dim),
            block(kv_local, slots, head_dim),
            block(kv_local, slots, head_dim),
        ],
        out_specs=block(kv_local, query_rows, head_dim),
        compiler_params=pltpu.CompilerParams(vmem_limit_bytes=VMEM_BYTES),
    )(lengths, q, entries, keys, values)


def angles(positions, steps, head_dim):
    freq_index = jnp.arange(head_dim // 2, dtype=jnp.float32)
    inverse_freq = jnp.exp(freq_index * (-2.0 * math.log(500000.0) / head_dim))
    step_pos = positions[None, :] + jnp.arange(steps, dtype=jnp.int32)[:, None]
    phase = step_pos.astype(jnp.float32)[..., None] * inverse_freq
    return jnp.cos(phase), jnp.sin(phase)


def body(n, hidden, w_query, key_value_weight, w_out, cache_keys, stored_values, lengths, positions):
    steps, row_local, depth = hidden.shape
    kv_local, head_dim = cache_keys.shape[1], cache_keys.shape[3]
    rows = steps * row_local
    ny = 2 if n == 8 else 1
    chunks = 4
    heads_local = w_out.shape[0] // head_dim
    group = heads_local // kv_local
    half = n // 2

    cosine, sine = angles(positions, steps, head_dim)
    tab = jnp.concatenate([cosine, cosine, -sine, sine], axis=-1).reshape(rows, 2 * head_dim)
    x = hidden.reshape(rows, 2, chunks, depth // (2 * chunks)).transpose(2, 1, 0, 3)
    x = x.reshape(chunks, 2 * rows, depth // (2 * chunks))
    kvcols = key_value_weight.shape[1]
    w_kv = key_value_weight
    if kvcols % 128:
        w_kv = jnp.pad(w_kv, ((0, 0), (0, 128 - kvcols % 128)))
    q, kv = project(ny, n, x, tab, w_query, w_kv)

    kv = kv[:, :, :kvcols].transpose(1, 0, 2).reshape(steps, row_local, kv_local, 2, head_dim)
    key, value = kv[:, :, :, 0], kv[:, :, :, 1]
    lower, upper = key[..., : head_dim // 2], key[..., head_dim // 2 :]
    cosine, sine = cosine[:, :, None], sine[:, :, None]
    key = jnp.concatenate([lower * cosine - upper * sine, upper * cosine + lower * sine], axis=-1)
    entries = jnp.stack([key, value], axis=3).astype(jnp.bfloat16)

    q = q.reshape(kv_local, group, steps, row_local, head_dim).transpose(3, 0, 2, 1, 4)
    q = q.reshape(row_local, kv_local, steps * group, head_dim)
    fresh = entries.transpose(1, 2, 3, 0, 4).reshape(row_local, kv_local, 2 * steps, head_dim)
    attended = attend(lengths, q, fresh.astype(jnp.float32), cache_keys, stored_values)

    wide = heads_local * head_dim
    a = attended.reshape(row_local, kv_local, steps, group * head_dim).transpose(2, 0, 1, 3)
    a = a.reshape(rows, 2, chunks, wide // (2 * chunks)).transpose(2, 1, 0, 3)
    a = a.reshape(chunks, 2 * rows, wide // (2 * chunks))
    out = mix(ny, n, a, w_out)
    out = out.reshape(n, steps, row_local, -1).transpose(1, 0, 2, 3)
    return out.reshape(steps, n * row_local, -1), entries


def solution(mesh):
    placed = (
        P(None, ("grp", "yz"), "gx"),
        P("gx", "yz"),
        P("gx", "yz"),
        P("gx", "yz"),
        P(("grp", "yz"), "gx", None, None),
        P(("grp", "yz"), "gx", None, None),
        P(("grp", "yz")),
        P(("grp", "yz")),
    )
    return jax.shard_map(
        functools.partial(body, mesh.shape["yz"]),
        mesh=mesh,
        in_specs=placed,
        out_specs=(P(None, "grp", ("yz", "gx")), P(None, ("grp", "yz"), "gx", None, None)),
        check_vma=False,
    )
```

time: 543 us -> 121 us (0.22); the launches traced: 537 us -> 121 us
  local copies, waits for them, and re-layouts: 253 us -> 10.9 us
  waiting for transfers between devices: 116 us -> 0 us
  Pallas kernels: 0 us -> 107 us
  blocking collectives: 65.5 us -> 0 us
  matrix products: 55.1 us -> 0 us
  starting transfers between devices: 20.1 us -> 0 us
  between operations: 14.7 us -> 0.75 us
  other arithmetic: 12.1 us -> 1.85 us
    unnamed x50 -> x4, local copies, waits for them, and re-layouts: 242 us -> 2.05 us
    pallas_call x0 -> x3, Pallas kernels: none -> 107 us  [the longest x1 56.8 us: project(): pl.pallas_call(functools.partial(project_kernel, ny, n), out_shape=(jax.S...]
    all_gather x2 -> x0, waiting for transfers between devices: 99.1 us -> none  [body(): lax.all_gather(hidden[step_index:step_index + 1], 'yz', axis=1, tiled=True)]
    all_gather x2 -> x0, blocking collectives: 65.5 us -> none  [body(): lax.all_gather(attended, 'yz', axis=1, tiled=True)]
    dot_general x13 -> x0, matrix products: 55.1 us -> none  [the longest x2 22.1 us: body(): jnp.einsum('snd,dc->snc', project_segment, w_query, preferred_element_typ...]
    all_to_all x4 -> x0, starting transfers between devices: 19 us -> none  [the longest x2 11 us: body(): lax.all_to_all(query_part, 'yz', split_axis=1, concat_axis=2, tiled=True)]
    reduce_scatter x2 -> x0, waiting for transfers between devices: 13.6 us -> none  [body(): lax.psum_scatter(mixed_cols, 'gx', scatter_dimension=2, tiled=True)]
    slice x5 -> x2, local copies, waits for them, and re-layouts: 6.19 us -> 0.05 us  [body(): key, value = (kv[:, :, :, 0], kv[:, :, :, 1])]
  transfers between devices with their start and end apart: 12 -> 0, of which waited for: 4 -> 0; matrix products, arithmetic and copies ran while one was open for 49% -> 0% of each run, Pallas kernels for 0% -> 0%
where the time goes in v1:
time: 121 us
  Pallas kernels  107 us (88%)
  local copies, waits for them, and re-layouts  10.9 us (9%)
  other arithmetic  1.85 us (2%)
    pallas_call x1, Pallas kernels, project(): pl.pallas_call(functools.partial(project_kernel, ny, n), out_shape=(jax.S...  56.8 us
    pallas_call x1, Pallas kernels, mix(): pl.pallas_call(functools.partial(mix_kernel, ny, n), out_shape=jax.ShapeD...  39.8 us
    pallas_call x1, Pallas kernels, attend(): pl.pallas_call(attend_kernel, grid=(rows // per_step,), out_shape=jax.Sha...  10.5 us

profile of v1, /device:TPU:1, one launch (start us, length us, event | category | flops | bytes accessed | tf_op | source)
XLA Modules:
  0.0 120.6 jit_solution(2590703491261776568)
XLA Ops:
  0.6 1.2 %copy.15 = bf16[2,12,8192]{2,1,0:T(8,128)(2,1)S(1)} copy(bf16[2,12,8192]{2,0,1:T(2,128)(2,1)} %param.8) | data formatting | bytes 786432 | tf_op args[0]
  1.9 0.3 reshape.80
  2.2 1.0 copy.16
  3.1 0.7 add.31
  4.0 0.1 multiply_cosine_fusion.1
  4.1 0.7 pad_maximum_fusion.tab
  4.8 56.8 %shard_map.95 = (bf16[4,192,128]{2,1,0:T(8,128)(2,1)}, f32[4,24,128]{2,1,0:T(8,128)}) custom-call(bf16[4,48,1024]{2,1,0:T(8,128)(2,1)} %bitcast.26, f32[24,256]{1,0:T(8,128)} %pad_maximum_fusion.tab, bf16[8192,1024]{1,0:T(8,128)(2,1)} %w_q.1, bf16[8192,128]{1,0:T(8,128)(2,1)} %w_kv.1), custom_call_target="tpu_custom_call" | custom-call | flops 3623878656 | bytes 18874368 | tf_op jit(solution)/shard_map/pallas_call | solution.py:280
  61.6 1.0 reshape.82
  62.6 0.8 copy.17
  63.3 0.8 copy.18
  64.2 0.1 multiply_cosine_fusion
  64.4 0.1 subtract_convert_fusion
  64.5 0.1 maximum_bitcast_fusion
  64.6 0.7 convert_bitcast_fusion
  65.3 0.6 copy.20
  65.9 10.5 %shard_map.96 = bf16[12,2,32,128]{3,2,1,0:T(8,128)(2,1)} custom-call(s32[12]{0:T(128)} %lengths.1, bf16[12,2,32,128]{3,2,1,0:T(8,128)(2,1)} %bitcast.29, f32[12,2,4,128]{3,2,1,0:T(4,128)} %bitcast.33, bf16[12,2,512,128]{3,2,1,0:T(8,128)(2,1)} %keys.1, bf16[12,2,512,128]{3,2,1,0:T(8,128)(2,1)} %values.1), custom_call_target="tpu_custom_call" | custom-call | tf_op jit(solution)/shard_map/pallas_call | solution.py:442
  76.4 1.0 reshape.85
  77.4 0.2 copy.26
  77.6 0.1 reshape.86
  77.7 0.7 copy.22
  78.4 39.8 %shard_map.97 = bf16[192,1024]{1,0:T(8,128)(2,1)} custom-call(bf16[4,48,512]{2,1,0:T(8,128)(2,1)} %bitcast.28, bf16[4096,2048]{1,0:T(8,128)(2,1)} %w.1), custom_call_target="tpu_custom_call" | custom-call | flops 3221225472 | bytes 16777216 | tf_op jit(solution)/shard_map/pallas_call | solution.py:375
  118.3 1.1 reshape.88
  119.4 0.4 copy.23
  119.8 0.8 copy.24
  (11 shorter events, 0.3 us)
Async XLA Ops:
  4.8 59.4 %copy-start = (s32[12]{0:T(128)S(1)}, s32[12]{0:T(128)}, u32[]{:S(2)}) copy-start(s32[12]{0:T(128)} %param.15) | copy-start | bytes 148

commit v2 on v0

v2 whole, which is shorter than its diff:
```python
import functools
import math

import jax
import jax.numpy as jnp
from jax import lax
from jax.experimental import pallas as pl
from jax.experimental.pallas import tpu as pltpu
from jax.sharding import PartitionSpec as P

MESH = pl.DeviceIdType.MESH
VMEM_BYTES = 60 * 1024 * 1024
F32, BF16 = jnp.float32, jnp.bfloat16


def remote(src, dst, send, recv, **where):
    return pltpu.make_async_remote_copy(
        src_ref=src, dst_ref=dst, send_sem=send, recv_sem=recv, device_id=where, device_id_type=MESH
    )


def start(copy):
    copy.start()


def enter(n):
    me, core = lax.axis_index("yz"), lax.axis_index("gx")
    barrier = pltpu.get_barrier_semaphore()
    for k in range(1, 2 * n):
        there = lax.rem(me * 2 + core + k, 2 * n)
        pl.semaphore_signal(
            barrier,
            inc=1,
            device_id={"yz": lax.div(there, 2), "gx": lax.rem(there, 2)},
            device_id_type=MESH,
        )
    pl.semaphore_wait(barrier, 2 * n - 1)


class Gather:
    def __init__(self, ny, n, blocks, y_first, send, recv):
        self.ny, self.nz, self.n = ny, n // ny, n
        self.blocks, self.send, self.recv = blocks, send, recv
        self.y_first = y_first if ny == 2 else ()
        self.me = lax.axis_index("yz")
        self.z, self.y = lax.div(self.me, ny), lax.rem(self.me, ny)

    def copy(self, c, d, way):
        to = (self.me + 1 - 2 * self.y, self.me + self.ny, self.me - self.ny)[way]
        block = self.blocks[c].at[d]
        return remote(block, block, self.send.at[c, d, way], self.recv.at[c, d], yz=to)

    def await_block(self, c, d):
        block = self.blocks[c].at[d]
        remote(block, block, self.send.at[c, d, 0], self.recv.at[c, d], yz=self.me).wait_recv()

    def both_ways(self, c, d, act):
        @pl.when(self.z + 1 < self.nz)
        def _():
            act(self.copy(c, d, 1))

        @pl.when(self.z > 0)
        def _():
            act(self.copy(c, d, 2))

    def own(self, c, act):
        if c in self.y_first:
            act(self.copy(c, self.me, 0))
        self.both_ways(c, self.me, act)
        if self.ny == 2 and c not in self.y_first:
            act(self.copy(c, self.me, 0))

    def partner(self, c, act, wait):
        if c in self.y_first:
            d = self.z * 2 + 1 - self.y
            if wait:
                self.await_block(c, d)
            self.both_ways(c, d, act)

    def hop(self, c, s, act, wait):
        for sign in (1, -1):
            origin = self.z - sign * s
            onward = self.z + sign

            @pl.when((origin >= 0) & (origin < self.nz))
            def _():
                columns = (self.y, 1 - self.y) if c in self.y_first else (self.y,)
                for y in columns:
                    d = origin * self.ny + y
                    if wait:
                        self.await_block(c, d)

                    @pl.when((onward >= 0) & (onward < self.nz))
                    def _():
                        act(self.copy(c, d, 1 if sign > 0 else 2))

                    if self.ny == 2 and c not in self.y_first:
                        act(self.copy(c, d, 0))

    def across(self, c):
        if self.ny == 2 and c not in self.y_first:
            for z in range(self.nz):
                self.await_block(c, z * 2 + 1 - self.y)

    def finish(self):
        for c in range(len(self.blocks)):
            self.own(c, lambda copy: copy.wait_send())
            self.partner(c, lambda copy: copy.wait_send(), False)
            for s in range(1, self.nz):
                self.hop(c, s, lambda copy: copy.wait_send(), False)

    def steps(self, c):
        todo = [functools.partial(self.partner, c, start, True)] if c in self.y_first else []
        return todo + [
            functools.partial(self.hop, c, s, start, True) for s in range(1, self.nz)
        ]

    def weave(self, steps, work):
        steps, work = list(steps), list(work)
        each = -(-len(work) // max(1, len(steps)))
        for step in steps:
            step()
            for piece in work[:each]:
                piece()
            work = work[each:]
        for piece in work:
            piece()


def stacked(blocks, c, first, count, half):
    rows = blocks[c].shape[1] // 2
    block = blocks[c][pl.ds(first, count)].astype(F32)[:, half * rows : (half + 1) * rows, :]
    return block.reshape(count * rows, blocks[c].shape[2]).astype(BF16)


def kernel(
    ny, n, widths, y_first, widths2, y_first2, kv_cols, *refs
):
    (hid, freq, pos, lens, w_q, w_kv, w_o, keys_hbm, values_hbm, out, entries_out) = refs[:11]
    count, count2 = len(widths), len(widths2)
    blocks, blocks2 = refs[11 : 11 + count], refs[11 + count : 11 + count + count2]
    (
        wq, wkv, wo, keys, values, lhs, stage, tab, tabs, acc_q, acc_kv, got_q, got_kv,
        q_send, kv_send, q_recv, kv_recv, qf, af, ent, acc, got, wide,
        send, recv, send2, recv2, w_sem, o_sem, cache_sem, t_send, t_recv, p_send, p_recv,
        a_send, a_recv, s_send, s_recv,
    ) = refs[11 + count + count2 :]
    me, core = lax.axis_index("yz"), lax.axis_index("gx")
    half = n // 2
    steps, row_local = hid.shape[0], hid.shape[1]
    rows = steps * row_local
    mine, other = core * half, (1 - core) * half
    side, slot = lax.div(me, half), lax.rem(me, half)
    heads = wq.shape[1] // 128
    kv_local = keys.shape[1]
    group = half * heads // kv_local

    starts, starts2 = [0], [0]
    for w in widths:
        starts.append(starts[-1] + 2 * w)
    for w in widths2:
        starts2.append(starts2[-1] + 2 * w)

    def weight(c, which):
        part = pl.ds(starts[c], 2 * widths[c])
        src, dst = ((w_q, wq), (w_kv, wkv))[which]
        return pltpu.make_async_copy(src.at[part], dst.at[part], w_sem.at[c, which])

    def out_weight(c):
        part = pl.ds(starts2[c], 2 * widths2[c])
        return pltpu.make_async_copy(w_o.at[part], wo.at[part], o_sem.at[c])

    def cache(which):
        src, dst = ((keys_hbm, keys), (values_hbm, values))[which]
        return pltpu.make_async_copy(src, dst, cache_sem.at[which])

    for c in range(count):
        for which in range(2):
            weight(c, which).start()

    gather = Gather(ny, n, blocks, y_first, send, recv)
    gather2 = Gather(ny, n, blocks2, y_first2, send2, recv2)

    def place(c):
        w = widths[c]
        for h in range(2):
            for s in range(steps):
                at = h * rows + s * row_local
                part = hid[s, :, starts[c] + h * w : starts[c] + (h + 1) * w]
                stage[at : at + row_local, :w] = part.astype(F32)
        blocks[c][me] = stage[:, :w].astype(BF16)

    place(0)
    enter(n)
    gather.own(0, start)
    place(1)
    gather.own(1, start)

    row = lax.broadcasted_iota(jnp.int32, (rows, 128), 0)
    step_pos = jnp.zeros((rows, 128), F32)
    for s in range(steps):
        for b in range(row_local):
            step_pos = jnp.where(row == s * row_local + b, (pos[b] + s).astype(F32), step_pos)
    phase = step_pos * freq[...]
    lower = lax.broadcasted_iota(jnp.int32, (rows, 128), 1) < 64
    sine = jnp.sin(phase)
    tab[:, :128] = jnp.cos(phase)
    tab[:, 128:] = jnp.where(lower, -sine, sine)

    def tab_copy(k):
        return remote(tab, tabs.at[slot], t_send.at[k - 1], t_recv.at[slot], yz=lax.rem(me + k, n))

    @pl.when(side == core)
    def _():
        tabs[slot] = tab[...]
        for k in range(1, n):
            tab_copy(k).start()

    for which in range(2):
        cache(which).start()
    for c in range(count2):
        out_weight(c).start()
    for c in range(2, count):
        place(c)

    def add(ref, c, at, value):
        if c == 0:
            ref[at] = value
        else:
            ref[at] += value

    def load_lhs(c):
        gather.across(c)
        for which in range(2):
            weight(c, which).wait()
        for h in range(2):
            lhs[h, :, : widths[c]] = stacked(blocks, c, 0, n, h)

    def times(first, left, ref, cols):
        total = None
        for h in range(2):
            w = left[h].shape[1]
            part = slice(first + h * w, first + (h + 1) * w)
            term = jnp.dot(left[h], ref[part, cols], preferred_element_type=F32)
            total = term if h == 0 else total + term
        return total

    def piece(c, acc_ref, ref, cols):
        left = [lhs[h, :, : widths[c]] for h in range(2)]
        add(acc_ref, c, (slice(None), cols), times(starts[c], left, ref, cols))

    qcols, kvw = wq.shape[1], wkv.shape[1]

    def pieces(c):
        cut = qcols // 2
        return [
            functools.partial(load_lhs, c),
            functools.partial(piece, c, acc_q, wq, slice(0, cut)),
            functools.partial(piece, c, acc_q, wq, slice(cut, qcols)),
            functools.partial(piece, c, acc_kv, wkv, slice(0, kvw)),
        ]

    for c in range(count):
        if c + 1 < count and c > 0:
            gather.own(c + 1, start)
        gather.weave(gather.steps(c), pieces(c - 1) if c > 0 else [])

    last = count - 1
    gather.across(last)
    for which in range(2):
        weight(last, which).wait()

    def last_part(first):
        left = [stacked(blocks, last, first, half, h) for h in range(2)]
        part = pl.ds(pl.multiple_of(first * rows, 8), half * rows)
        acc_q[part] += times(starts[last], left, wq, slice(0, qcols))
        acc_kv[part] += times(starts[last], left, wkv, slice(0, kvw))

    theirs = pl.ds(pl.multiple_of(other * rows, 8), half * rows)
    swap_q = remote(acc_q.at[theirs], got_q, p_send.at[0], p_recv.at[0], gx=1 - core)
    swap_kv = remote(acc_kv.at[theirs], got_kv, p_send.at[1], p_recv.at[1], gx=1 - core)
    last_part(other)
    swap_q.start()
    swap_kv.start()
    last_part(mine)

    for i in range(half):
        @pl.when(mine + i != me)
        def _():
            remote(tab, tabs.at[i], t_send.at[0], t_recv.at[i], yz=me).wait_recv()

    swap_q.wait_recv()
    swap_kv.wait_recv()

    def moved(i, which):
        src, dst = ((q_send, q_recv), (kv_send, kv_recv))[which]
        return remote(
            src.at[i], dst.at[slot], a_send.at[which, i], a_recv.at[which, slot], yz=mine + i, gx=side
        )

    for i in range(half):
        own_rows = pl.ds(pl.multiple_of((mine + i) * rows, 8), rows)
        got_rows = slice(i * rows, (i + 1) * rows)
        turned = []
        for head in range(heads):
            cols = slice(head * 128, (head + 1) * 128)
            u = acc_q[own_rows, cols] + got_q[got_rows, cols]
            turned.append(u * tabs[i, :, :128] + pltpu.roll(u, 64, 1) * tabs[i, :, 128:])
            if head % 2 == 1:
                pair = jnp.concatenate(turned[-2:], axis=0).astype(BF16)
                q_send[i, (head - 1) * rows : (head + 1) * rows, :] = pair
        kv_send[i] = acc_kv[own_rows, :] + got_kv[got_rows, :]
        here = (mine + i == me) & (side == core)

        @pl.when(jnp.logical_not(here))
        def _():
            moved(i, 0).start()
            moved(i, 1).start()

        @pl.when(here)
        def _():
            q_recv[slot] = q_send[i]
            kv_recv[slot] = kv_send[i]

    def await_moved(j):
        @pl.when(jnp.logical_not((mine + j == me) & (side == core)))
        def _():
            remote(q_send.at[0], q_recv.at[j], a_send.at[0, 0], a_recv.at[0, j], yz=me).wait_recv()
            remote(kv_send.at[0], kv_recv.at[j], a_send.at[1, 0], a_recv.at[1, j], yz=me).wait_recv()

    per_vector = 128 // kv_cols
    per_head = half // kv_local
    for which in range(2):
        cache(which).wait()
    for j in range(half):
        await_moved(j)
    for i in range(2 * kv_local):
        parts = [kv_recv[i * per_vector + k, :, :kv_cols] for k in range(per_vector)]
        u = parts[0] if per_vector == 1 else jnp.concatenate(parts, axis=1)
        if i % 2 == 0:
            u = u * tab[:, :128] + pltpu.roll(u, 64, 1) * tab[:, 128:]
        u = u.astype(BF16)
        entries_out[:, i * 128 : (i + 1) * 128] = u
        ent[i] = u.astype(F32)
    for j in range(half):
        qf[j * heads * rows : (j + 1) * heads * rows, :] = q_recv[j].astype(F32)

    query_rows = steps * group
    slots = keys.shape[2]
    scale = 128 ** (-0.5)
    at_slot = lax.broadcasted_iota(jnp.int32, (query_rows, slots), 1)
    first_step = lax.broadcasted_iota(jnp.int32, (query_rows, 1), 0) < group

    def attend(h, b):
        base = h * group * rows
        picked = [pl.ds(base + s * row_local + b, group, stride=rows) for s in range(steps)]
        query_wide = jnp.concatenate([qf[p, :] for p in picked], axis=0)
        scores = lax.dot_general(
            query_wide.astype(BF16), keys[b, h], (((1,), (1,)), ((), ())), preferred_element_type=F32
        ) * scale
        scores = jnp.where(at_slot < lens[b], scores, -jnp.inf)
        key0, key1 = ent[2 * h, pl.ds(b, 1), :], ent[2 * h, pl.ds(row_local + b, 1), :]
        value0 = ent[2 * h + 1, pl.ds(b, 1), :]
        value1 = ent[2 * h + 1, pl.ds(row_local + b, 1), :]
        new0 = jnp.sum(query_wide * key0, axis=1, keepdims=True) * scale
        new1 = jnp.sum(query_wide * key1, axis=1, keepdims=True) * scale
        new1 = jnp.where(first_step, -jnp.inf, new1)
        top = jnp.maximum(jnp.max(scores, axis=1, keepdims=True), jnp.maximum(new0, new1))
        grown = jnp.exp(scores - top)
        grown0, grown1 = jnp.exp(new0 - top), jnp.exp(new1 - top)
        total = jnp.sum(grown, axis=1, keepdims=True) + (grown0 + grown1)
        weights = (grown / total).astype(BF16)
        weight0 = (grown0 / total).astype(BF16).astype(F32)
        weight1 = (grown1 / total).astype(BF16).astype(F32)
        result = jnp.dot(weights, values[b, h], preferred_element_type=F32)
        result = result + (weight0 * value0 + weight1 * value1)
        for s in range(steps):
            af[picked[s], :] = result[s * group : (s + 1) * group]

    def attend_rows(h, first, stop):
        @pl.loop(first, stop)
        def _(b):
            attend(h, b)

    def place2(c):
        w = widths2[c]
        for k in range(w // 128):
            top, bottom = starts2[c] // 128 + k, (starts2[c] + w) // 128 + k
            pair = [af[j * rows : (j + 1) * rows, :] for j in (top, bottom)]
            blocks2[c][me, :, k * 128 : (k + 1) * 128] = jnp.concatenate(pair, axis=0).astype(BF16)

    def load_lhs2(c):
        gather2.across(c)
        out_weight(c).wait()
        for h in range(2):
            lhs[h, :, : widths2[c]] = stacked(blocks2, c, 0, n, h)

    cut = acc.shape[2]

    def piece2(c, at):
        left = [lhs[h, :, : widths2[c]] for h in range(2)]
        whose = core if at < 2 else 1 - core
        cols = pl.ds(pl.multiple_of((whose * 2 + at % 2) * cut, 128), cut)
        add(acc, c, at, times(starts2[c], left, wo, cols))

    def pieces2(c):
        return [functools.partial(load_lhs2, c)] + [
            functools.partial(piece2, c, at) for at in (2, 3, 0, 1)
        ]

    swap = [remote(acc.at[2 + k], got.at[k], s_send.at[k], s_recv.at[k], gx=1 - core) for k in range(2)]

    ready = 0

    def send_ready(units):
        nonlocal ready
        while ready < count2 and starts2[ready + 1] <= units * 128:
            place2(ready)
            gather2.own(ready, start)
            ready += 1

    third = -(-row_local // 4)
    for h in range(kv_local):
        passing = gather2.steps(0) if ready > 0 else []
        work = [
            functools.partial(attend_rows, h, k, min(k + third, row_local))
            for k in range(0, row_local, third)
        ]
        work[0]()
        if passing:
            gather2.weave(passing, work[1:])
        else:
            for part in work[1:]:
                part()
        send_ready((h + 1) * group)

    for c in range(1, count2):
        gather2.weave(gather2.steps(c), pieces2(c - 1))
    last = count2 - 1
    load_lhs2(last)
    for at in (2, 3):
        piece2(last, at)
        swap[at - 2].start()
    piece2(last, 0)
    piece2(last, 1)
    for k in range(2):
        swap[k].wait_recv()
        cols = slice(k * cut, (k + 1) * cut)
        for d in range(n):
            for s in range(steps):
                at = slice(d * rows + s * row_local, d * rows + (s + 1) * row_local)
                wide[s, d * row_local : (d + 1) * row_local, cols] = acc[k, at, :] + got[k, at, :]
    for s in range(steps):
        out[s] = wide[s].astype(BF16)

    gather.finish()
    gather2.finish()
    swap_q.wait_send()
    swap_kv.wait_send()
    for k in range(2):
        swap[k].wait_send()

    @pl.when(side == core)
    def _():
        for k in range(1, n):
            tab_copy(k).wait_send()

    for i in range(half):
        @pl.when(jnp.logical_not((mine + i == me) & (side == core)))
        def _():
            moved(i, 0).wait_send()
            moved(i, 1).wait_send()


def body(n, hidden, w_query, key_value_weight, w_out, cache_keys, stored_values, lengths, positions):
    steps, row_local, depth = hidden.shape
    kv_local, head_dim = cache_keys.shape[1], cache_keys.shape[3]
    rows = steps * row_local
    ny = 2 if n == 8 else 1
    half = n // 2
    depth2, width = w_out.shape
    kv_cols = key_value_weight.shape[1]
    w_kv = key_value_weight
    if kv_cols % 128:
        w_kv = jnp.pad(w_kv, ((0, 0), (0, 128 - kv_cols % 128)))
    qcols, kvw = w_query.shape[1], w_kv.shape[1]
    heads = qcols // 128
    heads_local = depth2 // 128

    units = depth // 256
    tail = max(1, units // 6)
    big = -(-(units - tail) // 3)
    widths = [128 * w for w in (big, big, units - tail - 2 * big, tail)]
    units = depth2 // 256
    tail = max(1, round(units / 6))
    widths2 = [128 * w for w in (units // 2, units - units // 2 - tail, tail)]

    freq_index = jnp.arange(head_dim // 2, dtype=F32)
    inverse_freq = jnp.exp(freq_index * (-2.0 * math.log(500000.0) / head_dim))
    freq = jnp.concatenate([inverse_freq, inverse_freq])[None, :]

    dma = pltpu.SemaphoreType.DMA
    vmem = pl.BlockSpec(memory_space=pltpu.VMEM)
    smem = pl.BlockSpec(memory_space=pltpu.SMEM)
    hbm = pl.BlockSpec(memory_space=pl.ANY)
    count, count2 = len(widths), len(widths2)
    blocks = [pltpu.VMEM((n, 2 * rows, w), BF16) for w in widths + widths2]
    scratch = blocks + [
        pltpu.VMEM(w_query.shape, BF16),
        pltpu.VMEM(w_kv.shape, BF16),
        pltpu.VMEM(w_out.shape, BF16),
        pltpu.VMEM(cache_keys.shape, BF16),
        pltpu.VMEM(stored_values.shape, BF16),
        pltpu.VMEM((2, n * rows, max(widths + widths2)), BF16),
        pltpu.VMEM((2 * rows, max(widths)), F32),
        pltpu.VMEM((rows, 256), F32),
        pltpu.VMEM((half, rows, 256), F32),
        pltpu.VMEM((n * rows, qcols), F32),
        pltpu.VMEM((n * rows, kvw), F32),
        pltpu.VMEM((half * rows, qcols), F32),
        pltpu.VMEM((half * rows, kvw), F32),
        pltpu.VMEM((half, heads * rows, 128), BF16),
        pltpu.VMEM((half, rows, kvw), F32),
        pltpu.VMEM((half, heads * rows, 128), BF16),
        pltpu.VMEM((half, rows, kvw), F32),
        pltpu.VMEM((heads_local * rows, 128), F32),
        pltpu.VMEM((heads_local * rows, 128), F32),
        pltpu.VMEM((2 * kv_local, rows, 128), F32),
        pltpu.VMEM((4, n * rows, width // 4), F32),
        pltpu.VMEM((2, n * rows, width // 4), F32),
        pltpu.VMEM((steps, n * row_local, width // 2), F32),
        dma((count, n, 3)),
        dma((count, n)),
        dma((count2, n, 3)),
        dma((count2, n)),
        dma((count, 2)),
        dma((count2,)),
        dma((2,)),
        dma((n - 1,)),
        dma((half,)),
        dma((2,)),
        dma((2,)),
        dma((2, half)),
        dma((2, half)),
        dma((2,)),
        dma((2,)),
    ]
    out, entries = pl.pallas_call(
        functools.partial(
            kernel, ny, n, widths, (count - 1,), widths2, (count2 - 1,), min(kv_cols, 128)
        ),
        out_shape=(
            jax.ShapeDtypeStruct((steps, n * row_local, width // 2), BF16),
            jax.ShapeDtypeStruct((rows, 2 * kv_local * 128), BF16),
        ),
        in_specs=[vmem, vmem, smem, smem, hbm, hbm, hbm, hbm, hbm],
        out_specs=(vmem, vmem),
        scratch_shapes=scratch,
        compiler_params=pltpu.CompilerParams(
            collective_id=0, has_side_effects=True, vmem_limit_bytes=VMEM_BYTES
        ),
    )(hidden, freq, positions, lengths, w_query, w_kv, w_out, cache_keys, stored_values)
    return out, entries.reshape(steps, row_local, kv_local, 2, head_dim)


def solution(mesh):
    placed = (
        P(None, ("grp", "yz"), "gx"),
        P("gx", "yz"),
        P("gx", "yz"),
        P("gx", "yz"),
        P(("grp", "yz"), "gx", None, None),
        P(("grp", "yz"), "gx", None, None),
        P(("grp", "yz")),
        P(("grp", "yz")),
    )
    return jax.shard_map(
        functools.partial(body, mesh.shape["yz"]),
        mesh=mesh,
        in_specs=placed,
        out_specs=(P(None, "grp", ("yz", "gx")), P(None, ("grp", "yz"), "gx", None, None)),
        check_vma=False,
    )
```

time: 543 us -> 107 us (0.20); the launches traced: 537 us -> 107 us
  local copies, waits for them, and re-layouts: 253 us -> 5.13 us
  waiting for transfers between devices: 116 us -> 0 us
  Pallas kernels: 0 us -> 100 us
  blocking collectives: 65.5 us -> 0 us
  matrix products: 55.1 us -> 0 us
  starting transfers between devices: 20.1 us -> 0 us
  between operations: 14.7 us -> 0.64 us
  other arithmetic: 12.1 us -> 0.6 us
    unnamed x50 -> x2, local copies, waits for them, and re-layouts: 242 us -> 3.77 us
    pallas_call x0 -> x1, Pallas kernels: none -> 100 us  [body(): pl.pallas_call(functools.partial(kernel, ny, n, widths, (count - 1,), wid...]
    all_gather x2 -> x0, waiting for transfers between devices: 99.1 us -> none  [body(): lax.all_gather(hidden[step_index:step_index + 1], 'yz', axis=1, tiled=True)]
    all_gather x2 -> x0, blocking collectives: 65.5 us -> none  [body(): lax.all_gather(attended, 'yz', axis=1, tiled=True)]
    dot_general x13 -> x0, matrix products: 55.1 us -> none  [the longest x2 22.1 us: body(): jnp.einsum('snd,dc->snc', project_segment, w_query, preferred_element_typ...]
    all_to_all x4 -> x0, starting transfers between devices: 19 us -> none  [the longest x2 11 us: body(): lax.all_to_all(query_part, 'yz', split_axis=1, concat_axis=2, tiled=True)]
    reduce_scatter x2 -> x0, waiting for transfers between devices: 13.6 us -> none  [body(): lax.psum_scatter(mixed_cols, 'gx', scatter_dimension=2, tiled=True)]
    slice x5 -> x0, local copies, waits for them, and re-layouts: 6.19 us -> none  [the longest x1 3.19 us: body(): hidden[step_index:step_index + 1]]
  transfers between devices with their start and end apart: 12 -> 0, of which waited for: 4 -> 0; matrix products, arithmetic and copies ran while one was open for 49% -> 0% of each run, Pallas kernels for 0% -> 0%
where the time goes in v2:
time: 107 us
  Pallas kernels  100 us (93%)
  local copies, waits for them, and re-layouts  5.13 us (5%)
    pallas_call x1, Pallas kernels, body(): pl.pallas_call(functools.partial(kernel, ny, n, widths, (count - 1,), wid...  100 us
    unnamed x2, local copies, waits for them, and re-layouts  3.77 us

profile of v2, /device:TPU:1, one launch (start us, length us, event | category | flops | bytes accessed | tf_op | source)
XLA Modules:
  0.0 106.6 jit_solution(6775249585858516035)
XLA Ops:
  0.6 0.6 maximum_bitcast_fusion.refs_1_
  1.2 2.0 %copy.10.refs_0_ = bf16[2,12,8192]{2,1,0:T(8,128)(2,1)} copy(bf16[2,12,8192]{2,0,1:T(2,128)(2,1)} %param.8) | data formatting | bytes 786432 | tf_op args[0]
  3.2 100.2 %shard_map.95 = (bf16[2,96,1024]{2,1,0:T(8,128)(2,1)}, bf16[24,512]{1,0:T(8,128)(2,1)}) custom-call(bf16[2,12,8192]{2,1,0:T(8,128)(2,1)} %copy.10.refs_0_, f32[1,128]{1,0:T(1,128)} %maximum_bitcast_fusion.refs_1_, s32[12]{0:T(128)} %refs_2_.1, s32[12]{0:T(128)} %refs_3_.1, bf16[8192,1024]{1,0:T(8,128)(2,1)} %refs_4_.1, bf16[8192,128]{1,0:T(8,128)(2,1)} %refs_5_.1, ...), custom_call_target="tpu_custom_call" | custom-call | tf_op jit(solution)/shard_map/pallas_call | solution.py:548
  103.5 1.4 %reshape.7 = bf16[2,12,2,2,128]{4,3,2,1,0:T(2,128)(2,1)} reshape(bf16[24,512]{1,0:T(8,128)(2,1)} %get-tuple-element.5) | data formatting | bytes 49152 | tf_op jit(solution)/shard_map/reshape | solution.py:563
  104.8 1.8 %copy.12 = bf16[2,96,1024]{2,1,0:T(8,128)(2,1)} copy(bf16[2,96,1024]{2,1,0:T(8,128)(2,1)} %get-tuple-element.8) | data formatting | bytes 786432
  (1 shorter events, 0.0 us)

commit v3 on v2

--- a/solution.py
+++ b/solution.py
@@ -174,10 +174,6 @@
         src, dst = ((keys_hbm, keys), (values_hbm, values))[which]
         return pltpu.make_async_copy(src, dst, cache_sem.at[which])
 
-    for c in range(count):
-        for which in range(2):
-            weight(c, which).start()
-
     gather = Gather(ny, n, blocks, y_first, send, recv)
     gather2 = Gather(ny, n, blocks2, y_first2, send2, recv2)
 
@@ -195,6 +191,8 @@
     gather.own(0, start)
     place(1)
     gather.own(1, start)
+    for which in range(2):
+        weight(0, which).start()
 
     row = lax.broadcasted_iota(jnp.int32, (rows, 128), 0)
     step_pos = jnp.zeros((rows, 128), F32)
@@ -216,10 +214,6 @@
         for k in range(1, n):
             tab_copy(k).start()
 
-    for which in range(2):
-        cache(which).start()
-    for c in range(count2):
-        out_weight(c).start()
     for c in range(2, count):
         place(c)
 
@@ -263,6 +257,15 @@
     for c in range(count):
         if c + 1 < count and c > 0:
             gather.own(c + 1, start)
+        if c + 1 < count:
+            for which in range(2):
+                weight(c + 1, which).start()
+        if c == 1:
+            for which in range(2):
+                cache(which).start()
+        if c == count - 1:
+            for k in range(count2):
+                out_weight(k).start()
         gather.weave(gather.steps(c), pieces(c - 1) if c > 0 else [])
 
     last = count - 1

time: 107 us -> 107 us (level)
  no operation moved by 1% of the time
where the time goes in v3:
time: 107 us
  Pallas kernels  100 us (93%)
  local copies, waits for them, and re-layouts  5.13 us (5%)
    pallas_call x1, Pallas kernels, body(): pl.pallas_call(functools.partial(kernel, ny, n, widths, (count - 1,), wid...  100 us
    unnamed x2, local copies, waits for them, and re-layouts  3.77 us

profile of v3, /device:TPU:1, one launch (start us, length us, event | category | flops | bytes accessed | tf_op | source)
XLA Modules:
  0.0 106.5 jit_solution(4391221656569316289)
XLA Ops:
  0.6 0.6 maximum_bitcast_fusion.refs_1_
  1.2 2.0 %copy.10.refs_0_ = bf16[2,12,8192]{2,1,0:T(8,128)(2,1)} copy(bf16[2,12,8192]{2,0,1:T(2,128)(2,1)} %param.8) | data formatting | bytes 786432 | tf_op args[0]
  3.2 100.1 %shard_map.95 = (bf16[2,96,1024]{2,1,0:T(8,128)(2,1)}, bf16[24,512]{1,0:T(8,128)(2,1)}) custom-call(bf16[2,12,8192]{2,1,0:T(8,128)(2,1)} %copy.10.refs_0_, f32[1,128]{1,0:T(1,128)} %maximum_bitcast_fusion.refs_1_, s32[12]{0:T(128)} %refs_2_.1, s32[12]{0:T(128)} %refs_3_.1, bf16[8192,1024]{1,0:T(8,128)(2,1)} %refs_4_.1, bf16[8192,128]{1,0:T(8,128)(2,1)} %refs_5_.1, ...), custom_call_target="tpu_custom_call" | custom-call | tf_op jit(solution)/shard_map/pallas_call | solution.py:551
  103.4 1.4 %reshape.7 = bf16[2,12,2,2,128]{4,3,2,1,0:T(2,128)(2,1)} reshape(bf16[24,512]{1,0:T(8,128)(2,1)} %get-tuple-element.5) | data formatting | bytes 49152 | tf_op jit(solution)/shard_map/reshape | solution.py:566
  104.7 1.8 %copy.12 = bf16[2,96,1024]{2,1,0:T(8,128)(2,1)} copy(bf16[2,96,1024]{2,1,0:T(8,128)(2,1)} %get-tuple-element.8) | data formatting | bytes 786432
  (1 shorter events, 0.0 us)
